TPU v7x, 32 devices: a whole 2x2x4 slice. The times are simulated.
32 devices in a mesh: run: 16 (over z, x, core), entry: 2 (over y).
Axes of the slice: x: 2, y: 2, z: 4, core: 2. Of those that a mesh axis runs over, the one named last changes fastest.
Arguments:
- gradients: bfloat16 [8192, 65536], P('run', 'entry'), may hold values from -6 to 6
- probes: bfloat16 [65536, 512], P(('entry', 'run')), may hold values from -0.0234375 to 0.0234375
Outputs:
- projected: float32 [512, 65536], P('run', 'entry')
All inputs are finite; a program needn't handle non-finite values.
Results may differ from a plain program's by a relative error of at most 0.0026.
Values may be sent and summed in bfloat16 or wider, within the bound.
A program may use at most 192 MiB of HBM per device.

v0:
```python
import jax
import jax.numpy as jnp
from jax import lax
from jax.sharding import PartitionSpec as P


def orthonormal(sketch, gram):
    factor = jnp.linalg.cholesky(gram)
    return lax.linalg.triangular_solve(
        factor, sketch, left_side=False, lower=True, transpose_a=True
    ).astype(jnp.bfloat16)


def per_device(gradients, probes):
    partial_sketch = jnp.dot(
        gradients,
        lax.all_gather(probes, "run", axis=0, tiled=True),
        preferred_element_type=jnp.float32,
    )
    sketch = lax.psum(partial_sketch, "entry")
    local_gram = jnp.dot(
        sketch.T, sketch, precision=lax.Precision.HIGHEST, preferred_element_type=jnp.float32
    )
    gram = lax.psum(local_gram, "run")
    basis = orthonormal(sketch, gram)
    return lax.psum_scatter(
        lax.dot_general(
            basis, gradients, (((0,), (0,)), ((), ())), preferred_element_type=jnp.float32
        ),
        "run",
        scatter_dimension=0,
        tiled=True,
    )


def solution(mesh):
    placed = (P("run", "entry"), P(("entry", "run"), None))
    return jax.shard_map(
        per_device, mesh=mesh, in_specs=placed, out_specs=P("run", "entry"), check_vma=False
    )
```

profile of v0, /device:TPU:0, one launch (start us, length us, event | category | flops | bytes accessed | tf_op | source)
XLA Modules:
  0.0 1173.2 jit_solution(4509367705491339992)
XLA Ops:
  6.5 0.7 all-gather.2.cloned.1.call-update
  7.3 172.4 %all-gather.2.cloned.1.call-done = bf16[32768,512]{1,0:T(8,128)(2,1)} async-done(((bf16[2048,512]{1,0:T(8,128)(2,1)}), bf16[32768,512]{1,0:T(8,128)(2,1)}) %all-gather.2.cloned.1.call-update) | async-done | bytes 33554448 | tf_op jit(solution)/shard_map/all_gather | solution.py:17
  179.7 27.7 %fusion.42 = f32[512,512]{1,0:T(8,128)} fusion(bf16[512,32768]{1,0:T(8,128)(2,1)} %param.2, bf16[32768,512]{1,0:T(8,128)(2,1)} %all-gather.2.cloned.1.call-done), kind=kOutput, calls=%fused_computation.78 | convolution fusion | flops 17179869184 | bytes 68157440 | tf_op jit(solution)/shard_map/dot_general | solution.py:15
  207.5 40.2 %all-reduce.4.cloned.1.call-done = f32[512,512]{1,0:T(8,128)} async-done(((f32[512,512]{1,0:T(8,128)}), f32[512,512]{1,0:T(8,128)}) %all-reduce.4.cloned.1.call-update) | async-done | bytes 1048592 | tf_op jit(solution)/shard_map/psum | solution.py:20
  247.7 4.4 fusion.43
  252.1 0.2 reduce-scatter.2.cloned.1.call-start
  252.3 93.2 %all-reduce.6.cloned.1.call-done = f32[512,512]{0,1:T(8,128)} async-done(((f32[512,512]{0,1:T(8,128)}), f32[512,512]{0,1:T(8,128)}) %all-reduce.6.cloned.1.call-update) | async-done | bytes 1048592 | tf_op jit(solution)/shard_map/psum | solution.py:24
  345.5 1.6 copy.4
  347.1 1.4 fusion
  348.6 11.7 cholesky.104
  360.3 9.8 custom-call.30
  370.1 0.1 cholesky.224
  370.3 0.3 constant_dynamic-update-slice_fusion.3
  370.6 0.3 convolution_subtract_fusion.3
  370.9 11.7 cholesky.217
  382.7 10.0 custom-call.31
  392.7 0.3 convolution_dynamic-update-slice_fusion
  393.0 0.4 convolution_subtract_fusion.4
  393.4 11.7 cholesky.238
  405.1 0.7 compare_reduce_fusion.1
  405.8 9.8 custom-call.32
  415.6 0.2 convolution_dynamic-update-slice_fusion.1
  415.8 0.4 convolution_subtract_fusion.5
  416.2 11.7 cholesky.255
  428.0 0.6 compare_reduce_fusion
  428.6 0.7 compare_reduce_fusion.2
  431.8 0.4 select_select_fusion
  432.2 8.5 while.1
  432.2 0.1 constant_dynamic-slice_fusion.2
  432.3 0.6 fusion.55
  432.9 1.4 bitcast_dynamic-update-slice_fusion.2
  434.4 0.6 fusion.55
  435.0 1.4 bitcast_dynamic-update-slice_fusion.2
  436.5 0.6 fusion.55
  437.1 1.4 bitcast_dynamic-update-slice_fusion.2
  438.6 0.1 constant_dynamic-slice_fusion.2
  438.7 0.6 fusion.55
  439.3 1.4 bitcast_dynamic-update-slice_fusion.2
  440.7 39.3 %custom-call.33 = f32[4,128,128]{1,2,0:T(8,128)S(1)} custom-call(f32[4,128,128]{2,1,0:T(8,128)S(1)} %get-tuple-element.12), custom_call_target="InvertDiagBlocksLowerTriangular" | custom-call | tf_op jit(solution)/shard_map/triangular_solve | solution.py:9
  480.0 1.4 fusion.41
  481.4 1.5 convolution_subtract_fusion.1
  483.0 0.4 fusion.40
  483.4 1.9 convolution_subtract_fusion
  485.3 0.4 fusion.39
  485.8 2.4 convolution_subtract_fusion.2
  488.2 0.4 convolution_convert_fusion
  488.6 41.1 %fusion.9 = f32[512,32768]{1,0:T(8,128)} fusion(bf16[512,32768]{1,0:T(8,128)(2,1)} %param.2, bf16[512,128]{0,1:T(8,128)(2,1)S(1)} %convolution_convert_fusion, bf16[512,128]{0,1:T(8,128)(2,1)S(1)} %get-tuple-element.35, bf16[512,128]{0,1:T(8,128)(2,1)S(1)} %get-tuple-element.37, bf16[512,128]{0,1:T(8,128)(2,1)S(1)} %get-tuple-element.39), kind=kOutput, calls=%fused_computation.23 | convolution fusion | flops 17181966336 | bytes 101187584 | tf_op jit(solution)/shard_map/dot_general | solution.py:27
  529.7 636.5 %reduce-scatter.2.cloned.1.call-done = f32[32,32768]{1,0:T(8,128)} async-done(((f32[512,32768]{1,0:T(8,128)}), f32[32,32768]{1,0:T(8,128)}) %reduce-scatter.2.cloned.1.call-update) | async-done | bytes 4194320 | tf_op jit(solution)/shard_map/reduce_scatter | solution.py:26
  (18 shorter events, 0.5 us)
Async XLA Ops:
  6.5 173.2 %all-gather.2.cloned.1.call-start = ((), (), s32[]{:S(2)}) async-start(), calls=%async_computation.1 | async-start | bytes 35651584 | tf_op jit(solution)/shard_map/all_gather | solution.py:17
  7.3 240.4 %all-reduce.4.cloned.1.call-start = ((), (), s32[]{:S(2)}) async-start(), calls=%async_computation.2 | async-start | bytes 2097152 | tf_op jit(solution)/shard_map/psum | solution.py:20
  207.5 138.1 %all-reduce.6.cloned.1.call-start = ((), (), s32[]{:S(2)}) async-start(), calls=%async_computation.3 | async-start | bytes 2097152 | tf_op jit(solution)/shard_map/psum | solution.py:24
  252.1 914.1 %reduce-scatter.2.cloned.1.call-start = ((), (), s32[]{:S(2)}) async-start(), calls=%async_computation.4 | async-start | bytes 71303168 | tf_op jit(solution)/shard_map/reduce_scatter | solution.py:26
Sparse Core Ops, SparseCore 0:
  9.0 170.7 all-gather.1
  207.6 40.0 all-reduce.3
  252.2 93.2 all-reduce.5
  529.9 636.3 reduce-scatter.1
where the time goes:
time: 1180 us; the launch traced here: 1170 us
  waiting for transfers between devices  943 us (80%)
  other arithmetic  120 us (10%)
  matrix products  83.6 us (7%)
  between operations  16.3 us (1%)
    reduce_scatter x1, waiting for transfers between devices, per_device(): lax.psum_scatter(lax.dot_general(basis, gradients, (((0,), (0,)), ((), ()...  636 us
    all_gather x1, waiting for transfers between devices, per_device(): lax.all_gather(probes, 'run', axis=0, tiled=True)  172 us
    psum x1, waiting for transfers between devices, per_device(): gram = lax.psum(local_gram, 'run')  93.2 us
    another operation x14, other arithmetic, orthonormal(): factor = jnp.linalg.cholesky(gram)  78.6 us
    dot_general x1, matrix products, per_device(): lax.dot_general(basis, gradients, (((0,), (0,)), ((), ())), preferred_ele...  41.1 us
    psum x1, waiting for transfers between devices, per_device(): sketch = lax.psum(partial_sketch, 'entry')  40.2 us
    another operation x3, other arithmetic, orthonormal(): lax.linalg.triangular_solve(factor, sketch, left_side=False, lower=True,...  39.7 us
    dot_general x1, matrix products, per_device(): jnp.dot(gradients, lax.all_gather(probes, 'run', axis=0, tiled=True), pre...  27.7 us
  transfers between devices with their start and end apart: 4, of which 4 were waited for; matrix products, arithmetic and copies ran while one was open for 0% of the time, Pallas kernels for 0%

commit v1 on v0

v1 whole, which is shorter than its diff:
```python
import functools

import jax
import jax.numpy as jnp
from jax import lax
from jax.experimental import pallas as pl
from jax.experimental.pallas import tpu as pltpu
from jax.sharding import PartitionSpec as P

HIGH = lax.Precision.HIGHEST
BLOCK = 128
TILE = 256
MESH = pl.DeviceIdType.MESH


def mm(a, b, dims, precision=None):
    return lax.dot_general(
        a, b, (dims, ((), ())), precision=precision, preferred_element_type=jnp.float32
    )


def factor_blocks(gram):
    count = gram.shape[0] // BLOCK
    eye = jnp.eye(BLOCK, dtype=jnp.float32)
    low, inv = {}, []
    rest = gram
    for k in range(count):
        diag = jnp.linalg.cholesky(rest[:BLOCK, :BLOCK], symmetrize_input=False)
        inverse = lax.linalg.triangular_solve(diag, eye, left_side=True, lower=True)
        inv.append(inverse)
        if k + 1 < count:
            panel = mm(rest[BLOCK:, :BLOCK], inverse, ((1,), (1,)), HIGH)
            for j in range(k + 1, count):
                low[j, k] = panel[(j - k - 1) * BLOCK : (j - k) * BLOCK]
            rest = rest[BLOCK:, BLOCK:] - mm(panel, panel, ((1,), (1,)), HIGH)
    return low, inv


def orthonormal(sketch, gram):
    low, inv = factor_blocks(gram)
    parts = []
    for k in range(len(inv)):
        right = sketch[:, k * BLOCK : (k + 1) * BLOCK]
        if k:
            row = jnp.concatenate([low[k, j] for j in range(k)], axis=1)
            right = right - mm(jnp.concatenate(parts, axis=1), row, ((1,), (1,)), HIGH)
        parts.append(mm(right, inv[k], ((1,), (1,)), HIGH))
    return jnp.concatenate(parts, axis=1).astype(jnp.bfloat16)


def project_kernel(
    depth, away_ref, home_ref, mine_ref, theirs_ref, out_ref,
    tiles, total, outgoing, incoming, relay,
    load_sem, x_send, x_recv, z_send, z_recv, keep_sem, core_send, core_recv,
):
    me = lax.axis_index("run")
    core, z = me % 2, me // 4
    flip = me + 1 - 2 * core
    across = me + 2 - 4 * ((me // 2) % 2)
    chunks, _, band, piece = total.shape
    rows = mine_ref.shape[0]
    last = depth - 1
    part = band // 2

    barrier = pltpu.get_barrier_semaphore()
    for device in (flip, across):
        pl.semaphore_signal(barrier, inc=1, device_id={"run": device}, device_id_type=MESH)

    @pl.when(z > 0)
    def _():
        pl.semaphore_signal(barrier, inc=1, device_id={"run": me - 4}, device_id_type=MESH)

    @pl.when(z < last)
    def _():
        pl.semaphore_signal(barrier, inc=1, device_id={"run": me + 4}, device_id_type=MESH)

    pl.semaphore_wait(barrier, 2 + (z + last - 1) // last + (2 * last - 1 - z) // last)

    def loads(k, slot):
        columns = pl.ds(pl.multiple_of(k * piece, piece), piece)
        return (
            pltpu.make_async_copy(
                mine_ref.at[:, columns], tiles.at[slot, pl.ds(0, rows)], load_sem.at[slot, 0]
            ),
            pltpu.make_async_copy(
                theirs_ref.at[:, columns], tiles.at[slot, pl.ds(rows, rows)], load_sem.at[slot, 1]
            ),
        )

    def x_copy(k):
        return pltpu.make_async_remote_copy(
            src_ref=outgoing.at[k], dst_ref=incoming.at[k],
            send_sem=x_send.at[k], recv_sem=x_recv.at[k],
            device_id={"run": across}, device_id_type=MESH,
        )

    def z_copy(k, slot, device):
        return pltpu.make_async_remote_copy(
            src_ref=relay.at[k, slot], dst_ref=relay.at[k, slot],
            send_sem=z_send.at[k, slot], recv_sem=z_recv.at[k, slot],
            device_id={"run": device}, device_id_type=MESH,
        )

    def result_copies(k):
        columns = pl.ds(pl.multiple_of((2 * k + core) * piece, piece), piece)
        keep = pltpu.make_async_copy(
            total.at[k, z, pl.ds(pl.multiple_of(core * part, part), part)],
            out_ref.at[:, columns], keep_sem.at[k],
        )
        give = pltpu.make_async_remote_copy(
            src_ref=total.at[k, z, pl.ds(pl.multiple_of((1 - core) * part, part), part)],
            dst_ref=out_ref.at[:, columns],
            send_sem=core_send.at[k], recv_sem=core_recv.at[k],
            device_id={"run": flip}, device_id_type=MESH,
        )
        return keep, give

    for copy in loads(0, 0):
        copy.start()

    def multiply(k, carry):
        slot = k % 2

        @pl.when(k + 1 < chunks)
        def _():
            for copy in loads(k + 1, 1 - slot):
                copy.start()

        for copy in loads(k, slot):
            copy.wait()

        def send_tile(i, carry):
            span = pl.ds(pl.multiple_of(i * TILE, TILE), TILE)
            value = jnp.dot(
                away_ref[...], tiles[slot, :, span], preferred_element_type=jnp.float32
            ).astype(jnp.bfloat16)
            for d in range(depth):
                outgoing[k, d, :, span] = value[d * band : (d + 1) * band]
            return carry

        def keep_tile(i, carry):
            span = pl.ds(pl.multiple_of(i * TILE, TILE), TILE)
            value = jnp.dot(home_ref[...], tiles[slot, :, span], preferred_element_type=jnp.float32)
            for d in range(depth):
                total[k, d, :, span] = value[d * band : (d + 1) * band]
            return carry

        lax.fori_loop(0, piece // TILE, send_tile, 0)
        x_copy(k).start()
        lax.fori_loop(0, piece // TILE, keep_tile, 0)
        return carry

    lax.fori_loop(0, chunks, multiply, 0)

    def pass_on(k, t, dest, slot, first, source, target):
        @pl.when(first)
        def _():
            relay[k, slot] = total[k, dest].astype(jnp.bfloat16)

        @pl.when(jnp.logical_not(first))
        def _():
            z_copy(k, slot, source).wait_recv()
            relay[k, slot] = (
                total[k, dest] + relay[k, slot].astype(jnp.float32)
            ).astype(jnp.bfloat16)

        z_copy(k, slot, target).start()

    def tick(now, carry):
        @pl.when(now < chunks)
        def _():
            x_copy(now).wait_recv()
            for d in range(depth):
                total[now, d] = total[now, d] + incoming[now, d].astype(jnp.float32)

        for t in range(last):
            k = now - t
            live = jnp.logical_and(k >= 0, k < chunks)

            @pl.when(jnp.logical_and(live, z <= t))
            def _():
                dest = last - t + z
                pass_on(k, t, dest, dest + 1, z == 0, me - 4, me + 4)

            @pl.when(jnp.logical_and(live, last - z <= t))
            def _():
                dest = t - last + z
                pass_on(k, t, dest, dest, z == last, me + 4, me - 4)

        @pl.when(now >= last)
        def _():
            k = now - last

            @pl.when(z > 0)
            def _():
                z_copy(k, z + 1, me - 4).wait_recv()
                total[k, z] = total[k, z] + relay[k, z + 1].astype(jnp.float32)

            @pl.when(z < last)
            def _():
                z_copy(k, z, me + 4).wait_recv()
                total[k, z] = total[k, z] + relay[k, z].astype(jnp.float32)

            for copy in result_copies(k):
                copy.start()

        return carry

    lax.fori_loop(0, chunks + last, tick, 0)

    def drain(k, carry):
        x_copy(k).wait_send()
        for t in range(last):
            @pl.when(z <= t)
            def _():
                z_copy(k, last - t + z + 1, me + 4).wait_send()

            @pl.when(last - z <= t)
            def _():
                z_copy(k, t - last + z, me - 4).wait_send()

        keep, give = result_copies(k)
        keep.wait()
        give.wait()
        return carry

    lax.fori_loop(0, chunks, drain, 0)


def project(depth, away, home, mine, theirs, piece):
    width, both = away.shape
    rows, columns = mine.shape
    chunks, band = columns // piece, width // depth
    any_space, vmem = pl.BlockSpec(memory_space=pl.ANY), pl.BlockSpec(memory_space=pltpu.VMEM)
    dma = pltpu.SemaphoreType.DMA
    return pl.pallas_call(
        functools.partial(project_kernel, depth),
        out_shape=jax.ShapeDtypeStruct((band // 2, 2 * columns), jnp.float32),
        in_specs=[vmem, vmem, any_space, any_space],
        out_specs=any_space,
        scratch_shapes=[
            pltpu.VMEM((2, both, piece), jnp.bfloat16),
            pltpu.VMEM((chunks, depth, band, piece), jnp.float32),
            pltpu.VMEM((chunks, depth, band, piece), jnp.bfloat16),
            pltpu.VMEM((chunks, depth, band, piece), jnp.bfloat16),
            pltpu.VMEM((chunks, depth + 1, band, piece), jnp.bfloat16),
            dma((2, 2)), dma((chunks,)), dma((chunks,)),
            dma((chunks, depth + 1)), dma((chunks, depth + 1)),
            dma((chunks,)), dma((chunks,)), dma((chunks,)),
        ],
        compiler_params=pltpu.CompilerParams(
            collective_id=0, has_side_effects=True, vmem_limit_bytes=60 * 2**20
        ),
        cost_estimate=pl.CostEstimate(
            flops=4 * width * both * columns, bytes_accessed=4 * rows * columns, transcendentals=0
        ),
    )(away, home, mine, theirs)


def solution(mesh):
    runs, entries = mesh.shape["run"], mesh.shape["entry"]
    depth = runs // 4

    def swap(value, bit, axis="run"):
        size = mesh.shape[axis]
        return lax.ppermute(value, axis, [(i, i ^ bit) for i in range(size)])

    def butterfly(value, axis):
        bit = 1
        while bit < mesh.shape[axis]:
            value = value + swap(value, bit, axis)
            bit *= 2
        return value

    def per_device(gradients, probes):
        me = lax.axis_index("run")
        core, x, z = me % 2, (me // 2) % 2, me // 4
        rows, columns = gradients.shape
        piece, width = probes.shape
        halves = runs // 2

        def columns_of(c):
            return jnp.concatenate(
                [
                    lax.dynamic_slice_in_dim(gradients, (2 * j + c) * piece, piece, 1)
                    for j in range(halves)
                ],
                axis=1,
            )

        theirs = swap(columns_of(1 - core), 1)
        mine = columns_of(core)
        groups = [list(range(c, runs, 2)) for c in range(2)]
        table = lax.all_gather(probes, "run", axis=0, tiled=True, axis_index_groups=groups)
        other = swap(mm(theirs, table, ((1,), (0,))), 1)
        sketch = mm(mine, table, ((1,), (0,))) + other
        sketch = butterfly(sketch, "entry")
        part = lax.axis_index("entry") % 2
        half = lax.dynamic_slice_in_dim(sketch, part * (width // 2), width // 2, 1)
        gram_half = butterfly(mm(sketch, half, ((0,), (0,)), HIGH), "run")
        far_half = swap(gram_half, 1, "entry")
        gram = jnp.concatenate(
            [
                jnp.where(part == 0, gram_half, far_half),
                jnp.where(part == 0, far_half, gram_half),
            ],
            axis=1,
        )
        basis = orthonormal(sketch, gram)
        basis_theirs = swap(basis, 1)

        band = width // depth // 2

        def bands(value, which):
            value = value.reshape(rows, depth, 2, band)
            return lax.dynamic_index_in_dim(value, which, 2, keepdims=False).reshape(
                rows, depth * band
            )

        both = jnp.concatenate
        away = both([bands(basis, 1 - x), bands(basis_theirs, 1 - x)]).T
        home = both([bands(basis, x), bands(basis_theirs, x)]).T
        return project(depth, away, home, mine, theirs, piece)

    placed = (P("run", "entry"), P(("entry", "run"), None))
    return jax.shard_map(
        per_device, mesh=mesh, in_specs=placed, out_specs=P("run", "entry"), check_vma=False
    )
```

time: 1180 us -> 715 us (0.61)
  waiting for transfers between devices: 943 us -> 289 us
  Pallas kernels: 0 us -> 223 us
  matrix products: 83.6 us -> 43 us
  local copies, waits for them, and re-layouts: 10.1 us -> 37.9 us
  other arithmetic: 120 us -> 94.6 us
    reduce_scatter x1 -> x0, waiting for transfers between devices: 636 us -> none  [per_device(): lax.psum_scatter(lax.dot_general(basis, gradients, (((0,), (0,)), ((), ()...]
    pallas_call x0 -> x1, Pallas kernels: none -> 223 us  [project(): pl.pallas_call(functools.partial(project_kernel, depth), out_shape=jax.Sh...]
    psum x2 -> x0, waiting for transfers between devices: 133 us -> none  [the longest x1 93.2 us: per_device(): gram = lax.psum(local_gram, 'run')]
    ppermute x0 -> x9, waiting for transfers between devices: none -> 115 us  [swap(): return lax.ppermute(value, axis, [(i, i ^ bit) for i in range(size)])]
    unnamed x0 -> x10, local copies, waits for them, and re-layouts: none -> 35.3 us
    dot_general x3 -> x16, matrix products: 73.2 us -> 41.8 us  [mm(): lax.dot_general(a, b, (dims, ((), ())), precision=precision, preferred_el...]
    another operation x17 -> x20, other arithmetic: 118 us -> 92 us  [the longest x12 49.9 us: factor_blocks(): diag = jnp.linalg.cholesky(rest[:BLOCK, :BLOCK], symmetrize_input=False)]
  transfers between devices with their start and end apart: 4 -> 10, of which waited for: 4 -> 9; matrix products, arithmetic and copies ran while one was open for 0% -> 7% of each run, Pallas kernels for 0% -> 0%
where the time goes in v1:
time: 715 us; the launch traced here: 708 us
  waiting for transfers between devices  289 us (40%)
  Pallas kernels  223 us (31%)
  other arithmetic  94.6 us (13%)
  matrix products  43 us (6%)
  local copies, waits for them, and re-layouts  37.9 us (5%)
  between operations  14 us (2%)
    pallas_call x1, Pallas kernels, project(): pl.pallas_call(functools.partial(project_kernel, depth), out_shape=jax.Sh...  223 us
    all_gather x1, waiting for transfers between devices, per_device(): lax.all_gather(probes, 'run', axis=0, tiled=True, axis_index_groups=groups)  174 us
    ppermute x9, waiting for transfers between devices, swap(): return lax.ppermute(value, axis, [(i, i ^ bit) for i in range(size)])  115 us
    another operation x12, other arithmetic, factor_blocks(): diag = jnp.linalg.cholesky(rest[:BLOCK, :BLOCK], symmetrize_input=False)  49.9 us
    another operation x8, other arithmetic, factor_blocks(): inverse = lax.linalg.triangular_solve(diag, eye, left_side=True, lower=True)  42 us
    dot_general x16, matrix products, mm(): lax.dot_general(a, b, (dims, ((), ())), precision=precision, preferred_el...  41.8 us
    unnamed x10, local copies, waits for them, and re-layouts  35.3 us
  transfers between devices with their start and end apart: 10, of which 9 were waited for; matrix products, arithmetic and copies ran while one was open for 7% of the time, Pallas kernels for 0%

profile of v1, /device:TPU:0, one launch (start us, length us, event | category | flops | bytes accessed | tf_op | source)
XLA Modules:
  0.0 707.6 jit_solution(5237770061614590834)
XLA Ops:
  6.5 0.7 all-gather.2.cloned.1.call-update
  7.3 5.1 dynamic-slice_dynamic-update-slice_fusion.7
  12.4 5.7 dynamic-slice_dynamic-update-slice_fusion.6
  18.1 6.9 dynamic-slice_dynamic-update-slice_fusion.5
  25.0 5.5 dynamic-slice_dynamic-update-slice_fusion.4
  30.6 2.5 dynamic-slice_dynamic-update-slice_fusion.3
  33.1 2.5 dynamic-slice_dynamic-update-slice_fusion.2
  35.6 2.5 dynamic-slice_dynamic-update-slice_fusion.1
  38.2 2.5 dynamic-slice_dynamic-update-slice_fusion
  41.1 25.1 %collective-permute-done.theirs_ref = bf16[512,16384]{1,0:T(8,128)(2,1)} collective-permute-done((bf16[512,16384]{1,0:T(8,128)(2,1)}, bf16[512,16384]{1,0:T(8,128)(2,1)}, u32[]{:S(2)}, u32[]{:S(2)}) %collective-permute-start) | collective-permute-done | bytes 16777248 | tf_op jit(solution)/shard_map/ppermute | solution.py:266
  66.2 173.6 %all-gather.2.cloned.1.call-done = bf16[16384,512]{1,0:T(8,128)(2,1)} async-done(((bf16[2048,512]{1,0:T(8,128)(2,1)}), bf16[16384,512]{1,0:T(8,128)(2,1)}) %all-gather.2.cloned.1.call-update) | async-done | bytes 16777232 | tf_op jit(solution)/shard_map/all_gather | solution.py:294
  239.8 16.4 %fusion.58 = f32[512,512]{1,0:T(8,128)S(1)} fusion(bf16[512,16384]{1,0:T(8,128)(2,1)} %collective-permute-done.theirs_ref, bf16[16384,512]{1,0:T(8,128)(2,1)} %all-gather.2.cloned.1.call-done), kind=kOutput, calls=%fused_computation.105 | convolution fusion | flops 8589934592 | bytes 34603008 | tf_op jit(solution)/shard_map/dot_general | solution.py:17
  256.3 16.6 %fusion.57 = f32[512,512]{1,0:T(8,128)S(1)} fusion(bf16[512,16384]{1,0:T(8,128)(2,1)} %get-tuple-element.8.mine_ref, bf16[16384,512]{1,0:T(8,128)(2,1)} %all-gather.2.cloned.1.call-done), kind=kOutput, calls=%fused_computation.104 | convolution fusion | flops 8589934592 | bytes 34603008 | tf_op jit(solution)/shard_map/dot_general | solution.py:17
  273.2 1.6 collective-permute-start.2
  274.8 24.1 %collective-permute-done.2 = f32[512,512]{1,0:T(8,128)S(1)} collective-permute-done((f32[512,512]{1,0:T(8,128)S(1)}, f32[512,512]{1,0:T(8,128)S(1)}, u32[]{:S(2)}, u32[]{:S(2)}) %collective-permute-start.2) | collective-permute-done | bytes 1048608 | tf_op jit(solution)/shard_map/ppermute | solution.py:266
  299.0 1.8 fusion.11
  300.9 1.9 collective-permute-done.3
  302.9 0.6 collective-permute-start.4
  303.5 13.4 %collective-permute-done.4 = f32[512,256]{1,0:T(8,128)S(1)} collective-permute-done((f32[512,256]{1,0:T(8,128)S(1)}, f32[512,256]{1,0:T(8,128)S(1)}, u32[]{:S(2)}, u32[]{:S(2)}) %collective-permute-start.4) | collective-permute-done | bytes 524320 | tf_op jit(solution)/shard_map/ppermute | solution.py:266
  317.1 13.1 %collective-permute-done.5 = f32[512,256]{1,0:T(8,128)S(1)} collective-permute-done((f32[512,256]{1,0:T(8,128)S(1)}, f32[512,256]{1,0:T(8,128)S(1)}, u32[]{:S(2)}, u32[]{:S(2)}) %collective-permute-start.5) | collective-permute-done | bytes 524320 | tf_op jit(solution)/shard_map/ppermute | solution.py:266
  330.3 1.6 collective-permute-start.6
  331.8 22.9 %collective-permute-done.6 = f32[512,256]{1,0:T(8,128)S(1)} collective-permute-done((f32[512,256]{1,0:T(8,128)S(1)}, f32[512,256]{1,0:T(8,128)S(1)}, u32[]{:S(2)}, u32[]{:S(2)}) %collective-permute-start.6) | collective-permute-done | bytes 524320 | tf_op jit(solution)/shard_map/ppermute | solution.py:266
  354.8 1.6 collective-permute-start.7
  356.3 12.3 %collective-permute-done.7 = f32[512,256]{1,0:T(8,128)S(1)} collective-permute-done((f32[512,256]{1,0:T(8,128)S(1)}, f32[512,256]{1,0:T(8,128)S(1)}, u32[]{:S(2)}, u32[]{:S(2)}) %collective-permute-start.7) | collective-permute-done | bytes 524320 | tf_op jit(solution)/shard_map/ppermute | solution.py:266
  368.7 11.7 %cholesky.75 = f32[128,128]{1,0:T(8,128)S(1)} custom-call(f32[128,128]{1,0:T(8,128)S(1)} %slice.79), custom_call_target="Cholesky" | custom-call | tf_op jit(solution)/shard_map/jit(cholesky)/cholesky | solution.py:28
  380.5 0.6 compare_reduce_fusion.3
  381.1 0.7 fusion.37
  381.8 9.8 %custom-call.8 = f32[1,128,128]{1,2,0:T(8,128)S(1)} custom-call(f32[1,128,128]{2,1,0:T(8,128)S(1)} %fusion.37), custom_call_target="InvertDiagBlocksLowerTriangular" | custom-call | tf_op jit(solution)/shard_map/triangular_solve/custom-call.0 | solution.py:29
  392.7 0.7 fusion.6
  393.4 12.1 %cholesky.86 = f32[128,128]{1,0:T(8,128)S(1)} custom-call(f32[128,128]{1,0:T(8,128)S(1)} %slice.83), custom_call_target="Cholesky" | custom-call | tf_op jit(solution)/shard_map/jit(cholesky)/cholesky | solution.py:28
  405.5 0.6 compare_reduce_fusion.2
  406.2 0.7 fusion.38
  406.8 9.8 %custom-call.9 = f32[1,128,128]{1,2,0:T(8,128)S(1)} custom-call(f32[1,128,128]{2,1,0:T(8,128)S(1)} %fusion.38), custom_call_target="InvertDiagBlocksLowerTriangular" | custom-call | tf_op jit(solution)/shard_map/triangular_solve/custom-call.0 | solution.py:29
  418.7 11.7 %cholesky.97 = f32[128,128]{1,0:T(8,128)S(1)} custom-call(f32[128,128]{1,0:T(8,128)S(1)} %slice.89), custom_call_target="Cholesky" | custom-call | tf_op jit(solution)/shard_map/jit(cholesky)/cholesky | solution.py:28
  430.5 0.6 compare_reduce_fusion.1
  431.1 0.7 fusion.39
  431.8 10.0 %custom-call.10 = f32[1,128,128]{1,2,0:T(8,128)S(1)} custom-call(f32[1,128,128]{2,1,0:T(8,128)S(1)} %fusion.39), custom_call_target="InvertDiagBlocksLowerTriangular" | custom-call | tf_op jit(solution)/shard_map/triangular_solve/custom-call.0 | solution.py:29
  442.3 1.0 fusion.7
  444.0 11.7 %cholesky.108 = f32[128,128]{1,0:T(8,128)S(1)} custom-call(f32[128,128]{1,0:T(8,128)S(1)} %convolution_subtract_fusion), custom_call_target="Cholesky" | custom-call | tf_op jit(solution)/shard_map/jit(cholesky)/cholesky | solution.py:28
  455.7 0.6 compare_reduce_fusion
  456.4 0.7 fusion.40
  457.1 9.8 %custom-call.11 = f32[1,128,128]{1,2,0:T(8,128)S(1)} custom-call(f32[1,128,128]{2,1,0:T(8,128)S(1)} %fusion.40), custom_call_target="InvertDiagBlocksLowerTriangular" | custom-call | tf_op jit(solution)/shard_map/triangular_solve/custom-call.0 | solution.py:29
  467.2 1.5 fusion
  469.3 1.7 collective-permute-done.8
  471.1 0.9 maximum_bitcast_fusion.1.home_ref
  472.0 0.9 maximum_bitcast_fusion.away_ref
  472.9 223.2 %shard_map.28 = f32[32,32768]{1,0:T(8,128)} custom-call(bf16[256,1024]{1,0:T(8,128)(2,1)} %maximum_bitcast_fusion.away_ref, bf16[256,1024]{1,0:T(8,128)(2,1)} %maximum_bitcast_fusion.1.home_ref, bf16[512,16384]{1,0:T(8,128)(2,1)} %get-tuple-element.8.mine_ref, bf16[512,16384]{1,0:T(8,128)(2,1)} %collective-permute-done.theirs_ref), custom_call_target="tpu_custom_call" | custom-call | flops 17179869184 | bytes 33554432 | tf_op jit(solution)/shard_map/pallas_call | solution.py:236
  696.1 4.5 copy.29
  (42 shorter events, 6.8 us)
Async XLA Ops:
  6.5 233.3 %all-gather.2.cloned.1.call-start = ((), (), s32[]{:S(2)}) async-start(), calls=%async_computation | async-start | bytes 18874368 | tf_op jit(solution)/shard_map/all_gather | solution.py:294
  7.3 23.3 %copy-start = (bf16[512,32768]{1,0:T(8,128)(2,1)S(1)}, bf16[512,32768]{1,0:T(8,128)(2,1)}, u32[]{:S(2)}) copy-start(bf16[512,32768]{1,0:T(8,128)(2,1)} %param.5) | copy-start | bytes 100663296
  40.7 25.5 %collective-permute-start = (bf16[512,16384]{1,0:T(8,128)(2,1)}, bf16[512,16384]{1,0:T(8,128)(2,1)}, u32[]{:S(2)}, u32[]{:S(2)}) collective-permute-start(bf16[512,16384]{1,0:T(8,128)(2,1)} %get-tuple-element.6), channel_id=1, source_target_pairs={{0,2},{2,0},{4,6},{6,4},{8,10},{10,8},{12,14},{14,12},{16,18},{18,... | collective-permute-start | bytes 50331656 | tf_op jit(solution)/shard_map/ppermute | solution.py:266
  256.3 16.7 %collective-permute-start.1 = (f32[512,512]{1,0:T(8,128)S(1)}, f32[512,512]{1,0:T(8,128)S(1)}, u32[]{:S(2)}, u32[]{:S(2)}) collective-permute-start(f32[512,512]{1,0:T(8,128)S(1)} %fusion.58), channel_id=1, source_target_pairs={{0,2},{2,0},{4,6},{6,4},{8,10},{10,8},{12,14},{14,12},{16,18},{18,... | collective-permute-start | bytes 3145736 | tf_op jit(solution)/shard_map/ppermute | solution.py:266
  273.2 25.6 %collective-permute-start.2 = (f32[512,512]{1,0:T(8,128)S(1)}, f32[512,512]{1,0:T(8,128)S(1)}, u32[]{:S(2)}, u32[]{:S(2)}) collective-permute-start(f32[512,512]{1,0:T(8,128)S(1)} %add.175), channel_id=1, source_target_pairs={{0,1},{1,0},{2,3},{3,2},{4,5},{5,4},{6,7},{7,6},{8,9},{9,8},{10,11... | collective-permute-start | bytes 3145736 | tf_op jit(solution)/shard_map/ppermute | solution.py:266
  300.9 2.0 collective-permute-start.3
  302.9 14.0 %collective-permute-start.4 = (f32[512,256]{1,0:T(8,128)S(1)}, f32[512,256]{1,0:T(8,128)S(1)}, u32[]{:S(2)}, u32[]{:S(2)}) collective-permute-start(f32[512,256]{1,0:T(8,128)S(1)} %add.179), channel_id=1, source_target_pairs={{0,4},{2,6},{4,0},{6,2},{8,12},{10,14},{12,8},{14,10},{16,20},{18,... | collective-permute-start | bytes 1572872 | tf_op jit(solution)/shard_map/ppermute | solution.py:266
  317.0 13.2 %collective-permute-start.5 = (f32[512,256]{1,0:T(8,128)S(1)}, f32[512,256]{1,0:T(8,128)S(1)}, u32[]{:S(2)}, u32[]{:S(2)}) collective-permute-start(f32[512,256]{1,0:T(8,128)S(1)} %add.180), channel_id=1, source_target_pairs={{0,8},{2,10},{4,12},{6,14},{8,0},{10,2},{12,4},{14,6},{16,24},{18,... | collective-permute-start | bytes 1572872 | tf_op jit(solution)/shard_map/ppermute | solution.py:266
  330.3 24.4 %collective-permute-start.6 = (f32[512,256]{1,0:T(8,128)S(1)}, f32[512,256]{1,0:T(8,128)S(1)}, u32[]{:S(2)}, u32[]{:S(2)}) collective-permute-start(f32[512,256]{1,0:T(8,128)S(1)} %add.181), channel_id=1, source_target_pairs={{0,16},{2,18},{4,20},{6,22},{8,24},{10,26},{12,28},{14,30},{16,0},... | collective-permute-start | bytes 1572872 | tf_op jit(solution)/shard_map/ppermute | solution.py:266
  354.8 13.9 %collective-permute-start.7 = (f32[512,256]{1,0:T(8,128)S(1)}, f32[512,256]{1,0:T(8,128)S(1)}, u32[]{:S(2)}, u32[]{:S(2)}) collective-permute-start(f32[512,256]{1,0:T(8,128)S(1)} %add.182), channel_id=1, source_target_pairs={{0,1},{1,0},{2,3},{3,2},{4,5},{5,4},{6,7},{7,6},{8,9},{9,8},{10,11... | collective-permute-start | bytes 1572872 | tf_op jit(solution)/shard_map/ppermute | solution.py:266
  469.1 2.0 collective-permute-start.8
Sparse Core Ops, SparseCore 0:
  9.5 230.2 all-gather.1

commit v2 on v1

--- a/solution.py
+++ b/solution.py
@@ -290,10 +290,8 @@
 
         theirs = swap(columns_of(1 - core), 1)
         mine = columns_of(core)
-        groups = [list(range(c, runs, 2)) for c in range(2)]
-        table = lax.all_gather(probes, "run", axis=0, tiled=True, axis_index_groups=groups)
-        other = swap(mm(theirs, table, ((1,), (0,))), 1)
-        sketch = mm(mine, table, ((1,), (0,))) + other
+        table = lax.all_gather(probes, "run", axis=0, tiled=True)
+        sketch = mm(gradients, table, ((1,), (0,)))
         sketch = butterfly(sketch, "entry")
         part = lax.axis_index("entry") % 2
         half = lax.dynamic_slice_in_dim(sketch, part * (width // 2), width // 2, 1)

time: 715 us -> 648 us (0.906)
  waiting for transfers between devices: 289 us -> 225 us
    all_gather x1, waiting for transfers between devices: 174 us -> 139 us  [per_device(): table = lax.all_gather(probes, 'run', axis=0, tiled=True)]
    ppermute x9 -> x8, waiting for transfers between devices: 115 us -> 85.3 us  [swap(): return lax.ppermute(value, axis, [(i, i ^ bit) for i in range(size)])]
    dot_general x16 -> x15, matrix products: 41.8 us -> 35.7 us  [mm(): lax.dot_general(a, b, (dims, ((), ())), precision=precision, preferred_el...]
  transfers between devices with their start and end apart: 10 -> 9, of which waited for: 9 -> 8; matrix products, arithmetic and copies ran while one was open for 7% -> 26% of each run, Pallas kernels for 0% -> 0%
where the time goes in v2:
time: 648 us; the launch traced here: 640 us
  waiting for transfers between devices  225 us (35%)
  Pallas kernels  223 us (34%)
  other arithmetic  94.3 us (15%)
  local copies, waits for them, and re-layouts  37.7 us (6%)
  matrix products  36.8 us (6%)
  between operations  14 us (2%)
  starting transfers between devices  8.9 us (1%)
    pallas_call x1, Pallas kernels, project(): pl.pallas_call(functools.partial(project_kernel, depth), out_shape=jax.Sh...  223 us
    all_gather x1, waiting for transfers between devices, per_device(): table = lax.all_gather(probes, 'run', axis=0, tiled=True)  139 us
    ppermute x8, waiting for transfers between devices, swap(): return lax.ppermute(value, axis, [(i, i ^ bit) for i in range(size)])  85.3 us
    another operation x12, other arithmetic, factor_blocks(): diag = jnp.linalg.cholesky(rest[:BLOCK, :BLOCK], symmetrize_input=False)  50.1 us
    another operation x8, other arithmetic, factor_blocks(): inverse = lax.linalg.triangular_solve(diag, eye, left_side=True, lower=True)  41.9 us
    dot_general x15, matrix products, mm(): lax.dot_general(a, b, (dims, ((), ())), precision=precision, preferred_el...  35.7 us
    unnamed x10, local copies, waits for them, and re-layouts  35.1 us
  transfers between devices with their start and end apart: 9, of which 8 were waited for; matrix products, arithmetic and copies ran while one was open for 26% of the time, Pallas kernels for 0%

profile of v2, /device:TPU:0, one launch (start us, length us, event | category | flops | bytes accessed | tf_op | source)
XLA Modules:
  0.0 639.8 jit_solution(15593149973852154456)
XLA Ops:
  6.5 0.7 all-gather.2.cloned.1.call-update
  7.3 5.1 dynamic-slice_dynamic-update-slice_fusion.7
  12.4 5.7 dynamic-slice_dynamic-update-slice_fusion.6
  18.2 6.6 %dynamic-slice_dynamic-update-slice_fusion.5 = (bf16[512,16384]{1,0:T(8,128)(2,1)}, bf16[512,16384]{1,0:T(8,128)(2,1)}) fusion(bf16[512,16384]{1,0:T(8,128)(2,1)} %get-tuple-element.19, bf16[512,32768]{1,0:T(8,128)(2,1)} %param.5, s32[]{:T(128)S(6)} %select_n.114, bf16[512,16384]{1,0:T(8,128)(2,1)} %get-tuple-element.20, s32[]{:T(128)S(6)} %select_n.106), kind=kLoop, calls=%fused_computation.5 | loop fusion | bytes 8388616
  24.8 5.7 dynamic-slice_dynamic-update-slice_fusion.4
  30.5 2.5 dynamic-slice_dynamic-update-slice_fusion.3
  33.0 2.5 dynamic-slice_dynamic-update-slice_fusion.2
  35.5 2.4 dynamic-slice_dynamic-update-slice_fusion.1
  38.0 2.5 dynamic-slice_dynamic-update-slice_fusion
  40.9 138.9 %all-gather.2.cloned.1.call-done = bf16[32768,512]{1,0:T(8,128)(2,1)} async-done(((bf16[2048,512]{1,0:T(8,128)(2,1)}), bf16[32768,512]{1,0:T(8,128)(2,1)}) %all-gather.2.cloned.1.call-update) | async-done | bytes 33554448 | tf_op jit(solution)/shard_map/all_gather | solution.py:293
  179.7 26.9 %fusion.57 = f32[512,512]{1,0:T(8,128)S(1)} fusion(bf16[512,32768]{1,0:T(8,128)(2,1)} %param.5, bf16[32768,512]{1,0:T(8,128)(2,1)} %all-gather.2.cloned.1.call-done), kind=kOutput, calls=%fused_computation.104 | convolution fusion | flops 17179869184 | bytes 68157440 | tf_op jit(solution)/shard_map/dot_general | solution.py:17
  206.7 1.5 collective-permute-start
  208.2 23.8 %collective-permute-done = f32[512,512]{1,0:T(8,128)S(1)} collective-permute-done((f32[512,512]{1,0:T(8,128)S(1)}, f32[512,512]{1,0:T(8,128)S(1)}, u32[]{:S(2)}, u32[]{:S(2)}) %collective-permute-start) | collective-permute-done | bytes 1048608 | tf_op jit(solution)/shard_map/ppermute | solution.py:266
  232.3 1.8 fusion.11
  234.2 1.9 collective-permute-done.1
  236.1 1.2 collective-permute-start.2
  237.3 12.8 %collective-permute-done.2 = f32[512,256]{1,0:T(8,128)S(1)} collective-permute-done((f32[512,256]{1,0:T(8,128)S(1)}, f32[512,256]{1,0:T(8,128)S(1)}, u32[]{:S(2)}, u32[]{:S(2)}) %collective-permute-start.2) | collective-permute-done | bytes 524320 | tf_op jit(solution)/shard_map/ppermute | solution.py:266
  250.2 1.6 collective-permute-start.3
  251.8 11.7 %collective-permute-done.3 = f32[512,256]{1,0:T(8,128)S(1)} collective-permute-done((f32[512,256]{1,0:T(8,128)S(1)}, f32[512,256]{1,0:T(8,128)S(1)}, u32[]{:S(2)}, u32[]{:S(2)}) %collective-permute-start.3) | collective-permute-done | bytes 524320 | tf_op jit(solution)/shard_map/ppermute | solution.py:266
  263.5 2.5 collective-permute-start.4
  266.0 21.9 %collective-permute-done.4 = f32[512,256]{1,0:T(8,128)S(1)} collective-permute-done((f32[512,256]{1,0:T(8,128)S(1)}, f32[512,256]{1,0:T(8,128)S(1)}, u32[]{:S(2)}, u32[]{:S(2)}) %collective-permute-start.4) | collective-permute-done | bytes 524320 | tf_op jit(solution)/shard_map/ppermute | solution.py:266
  288.0 1.5 collective-permute-start.5
  289.5 11.4 %collective-permute-done.5 = f32[512,256]{1,0:T(8,128)S(1)} collective-permute-done((f32[512,256]{1,0:T(8,128)S(1)}, f32[512,256]{1,0:T(8,128)S(1)}, u32[]{:S(2)}, u32[]{:S(2)}) %collective-permute-start.5) | collective-permute-done | bytes 524320 | tf_op jit(solution)/shard_map/ppermute | solution.py:266
  301.0 11.7 %cholesky.75 = f32[128,128]{1,0:T(8,128)S(1)} custom-call(f32[128,128]{1,0:T(8,128)S(1)} %slice.79), custom_call_target="Cholesky" | custom-call | tf_op jit(solution)/shard_map/jit(cholesky)/cholesky | solution.py:28
  312.8 0.6 compare_reduce_fusion.3
  313.4 0.7 fusion.37
  314.1 9.8 %custom-call.8 = f32[1,128,128]{1,2,0:T(8,128)S(1)} custom-call(f32[1,128,128]{2,1,0:T(8,128)S(1)} %fusion.37), custom_call_target="InvertDiagBlocksLowerTriangular" | custom-call | tf_op jit(solution)/shard_map/triangular_solve/custom-call.0 | solution.py:29
  324.6 0.7 fusion.6
  325.3 12.1 %cholesky.86 = f32[128,128]{1,0:T(8,128)S(1)} custom-call(f32[128,128]{1,0:T(8,128)S(1)} %slice.83), custom_call_target="Cholesky" | custom-call | tf_op jit(solution)/shard_map/jit(cholesky)/cholesky | solution.py:28
  337.4 0.6 compare_reduce_fusion.2
  338.0 0.7 fusion.38
  338.7 9.8 %custom-call.9 = f32[1,128,128]{1,2,0:T(8,128)S(1)} custom-call(f32[1,128,128]{2,1,0:T(8,128)S(1)} %fusion.38), custom_call_target="InvertDiagBlocksLowerTriangular" | custom-call | tf_op jit(solution)/shard_map/triangular_solve/custom-call.0 | solution.py:29
  349.5 11.7 %cholesky.97 = f32[128,128]{1,0:T(8,128)S(1)} custom-call(f32[128,128]{1,0:T(8,128)S(1)} %slice.89), custom_call_target="Cholesky" | custom-call | tf_op jit(solution)/shard_map/jit(cholesky)/cholesky | solution.py:28
  361.3 0.6 compare_reduce_fusion.1
  361.9 0.7 fusion.39
  362.6 9.8 %custom-call.10 = f32[1,128,128]{1,2,0:T(8,128)S(1)} custom-call(f32[1,128,128]{2,1,0:T(8,128)S(1)} %fusion.39), custom_call_target="InvertDiagBlocksLowerTriangular" | custom-call | tf_op jit(solution)/shard_map/triangular_solve/custom-call.0 | solution.py:29
  373.2 11.9 %cholesky.108 = f32[128,128]{1,0:T(8,128)S(1)} custom-call(f32[128,128]{1,0:T(8,128)S(1)} %convolution_subtract_fusion), custom_call_target="Cholesky" | custom-call | tf_op jit(solution)/shard_map/jit(cholesky)/cholesky | solution.py:28
  385.1 0.6 compare_reduce_fusion
  385.8 0.7 fusion.40
  386.4 9.8 %custom-call.11 = f32[1,128,128]{1,2,0:T(8,128)S(1)} custom-call(f32[1,128,128]{2,1,0:T(8,128)S(1)} %fusion.40), custom_call_target="InvertDiagBlocksLowerTriangular" | custom-call | tf_op jit(solution)/shard_map/triangular_solve/custom-call.0 | solution.py:29
  396.7 0.6 fusion.43
  397.7 1.0 fusion.7
  399.1 1.5 fusion
  401.6 1.7 collective-permute-done.6
  403.4 0.9 maximum_bitcast_fusion.away_ref
  404.2 0.9 maximum_bitcast_fusion.1.home_ref
  405.1 223.2 %shard_map.28 = f32[32,32768]{1,0:T(8,128)} custom-call(bf16[256,1024]{1,0:T(8,128)(2,1)} %maximum_bitcast_fusion.away_ref, bf16[256,1024]{1,0:T(8,128)(2,1)} %maximum_bitcast_fusion.1.home_ref, bf16[512,16384]{1,0:T(8,128)(2,1)} %get-tuple-element.8.mine_ref, bf16[512,16384]{1,0:T(8,128)(2,1)} %collective-permute-done.7.theirs_ref), custom_call_target="tpu_custom_call" | custom-call | flops 17179869184 | bytes 33554432 | tf_op jit(solution)/shard_map/pallas_call | solution.py:236
  628.3 4.5 copy.29
  (38 shorter events, 5.9 us)
Async XLA Ops:
  6.5 173.2 %all-gather.2.cloned.1.call-start = ((), (), s32[]{:S(2)}) async-start(), calls=%async_computation | async-start | bytes 35651584 | tf_op jit(solution)/shard_map/all_gather | solution.py:293
  7.3 23.2 %copy-start = (bf16[512,32768]{1,0:T(8,128)(2,1)S(1)}, bf16[512,32768]{1,0:T(8,128)(2,1)}, u32[]{:S(2)}) copy-start(bf16[512,32768]{1,0:T(8,128)(2,1)} %param.5) | copy-start | bytes 100663296
  40.4 364.6 %collective-permute-start.7 = (bf16[512,16384]{1,0:T(8,128)(2,1)}, bf16[512,16384]{1,0:T(8,128)(2,1)}, u32[]{:S(2)}, u32[]{:S(2)}) collective-permute-start(bf16[512,16384]{1,0:T(8,128)(2,1)} %get-tuple-element.6), channel_id=1, source_target_pairs={{0,2},{2,0},{4,6},{6,4},{8,10},{10,8},{12,14},{14,12},{16,18},{18,... | collective-permute-start | bytes 50331656 | tf_op jit(solution)/shard_map/ppermute | solution.py:266
  206.7 25.4 %collective-permute-start = (f32[512,512]{1,0:T(8,128)S(1)}, f32[512,512]{1,0:T(8,128)S(1)}, u32[]{:S(2)}, u32[]{:S(2)}) collective-permute-start(f32[512,512]{1,0:T(8,128)S(1)} %fusion.57), channel_id=1, source_target_pairs={{0,1},{1,0},{2,3},{3,2},{4,5},{5,4},{6,7},{7,6},{8,9},{9,8},{10,11... | collective-permute-start | bytes 3145736 | tf_op jit(solution)/shard_map/ppermute | solution.py:266
  234.1 2.0 collective-permute-start.1
  236.1 14.0 %collective-permute-start.2 = (f32[512,256]{1,0:T(8,128)S(1)}, f32[512,256]{1,0:T(8,128)S(1)}, u32[]{:S(2)}, u32[]{:S(2)}) collective-permute-start(f32[512,256]{1,0:T(8,128)S(1)} %add.144), channel_id=1, source_target_pairs={{0,4},{2,6},{4,0},{6,2},{8,12},{10,14},{12,8},{14,10},{16,20},{18,... | collective-permute-start | bytes 1572872 | tf_op jit(solution)/shard_map/ppermute | solution.py:266
  250.2 13.2 %collective-permute-start.3 = (f32[512,256]{1,0:T(8,128)S(1)}, f32[512,256]{1,0:T(8,128)S(1)}, u32[]{:S(2)}, u32[]{:S(2)}) collective-permute-start(f32[512,256]{1,0:T(8,128)S(1)} %add.145), channel_id=1, source_target_pairs={{0,8},{2,10},{4,12},{6,14},{8,0},{10,2},{12,4},{14,6},{16,24},{18,... | collective-permute-start | bytes 1572872 | tf_op jit(solution)/shard_map/ppermute | solution.py:266
  263.5 24.4 %collective-permute-start.4 = (f32[512,256]{1,0:T(8,128)S(1)}, f32[512,256]{1,0:T(8,128)S(1)}, u32[]{:S(2)}, u32[]{:S(2)}) collective-permute-start(f32[512,256]{1,0:T(8,128)S(1)} %add.146), channel_id=1, source_target_pairs={{0,16},{2,18},{4,20},{6,22},{8,24},{10,26},{12,28},{14,30},{16,0},... | collective-permute-start | bytes 1572872 | tf_op jit(solution)/shard_map/ppermute | solution.py:266
  288.0 12.9 %collective-permute-start.5 = (f32[512,256]{1,0:T(8,128)S(1)}, f32[512,256]{1,0:T(8,128)S(1)}, u32[]{:S(2)}, u32[]{:S(2)}) collective-permute-start(f32[512,256]{1,0:T(8,128)S(1)} %add.147), channel_id=1, source_target_pairs={{0,1},{1,0},{2,3},{3,2},{4,5},{5,4},{6,7},{7,6},{8,9},{9,8},{10,11... | collective-permute-start | bytes 1572872 | tf_op jit(solution)/shard_map/ppermute | solution.py:266
  401.3 2.0 collective-permute-start.6
Sparse Core Ops, SparseCore 0:
  9.0 170.7 all-gather.1
